TPU v7x, 256 devices: a whole 4x4x8 slice. The times are simulated.
256 devices in a mesh: lat: 32 (over y_lo, z, core), lon: 8 (over y_hi, x).
Axes of the slice: x: 4, y: 4 (y_hi: 2, y_lo: 2; y = y_hi * 2 + y_lo), z: 8, core: 2. Of those that a mesh axis runs over, the one named last changes fastest.
Arguments:
- cotangent: bfloat16 [384, 384, 1024], P(None, 'lat', 'lon'), may hold values from -6 to 6
- layer_input: bfloat16 [384, 384, 1024], P(None, 'lat', 'lon'), may hold values from -6 to 6
- filter_values: bfloat16 [3, 384, 4, 17], replicated, may hold values from -4 to 4
- weights: bfloat16 [3, 384, 384], replicated, may hold values from -0.1875 to 0.1875
- row_offset: int32 [384], replicated, may hold values from -3 to 0, as said below
- reach: int32 [384], replicated, may hold values from 1 to 9, as said below
Outputs:
- input_grad: bfloat16 [384, 384, 1024], P(None, 'lat', 'lon')
- weight_grad: float32 [3, 384, 384], replicated
Inputs may be any that keep to these rules, and one draw needn't show every extreme that they name: The support rows of output latitude o are o + row_offset[o] to o + row_offset[o] + 3. Taps d with |d| < reach[o] are used.
All inputs are finite; a program needn't handle non-finite values.
Results may differ from a plain program's by a relative error of at most 0.0049.
Values may be sent and summed in bfloat16 or wider, within the bound.
A program may use at most 128 MiB of HBM per device.

v0:
```python
import jax
import jax.numpy as jnp
from jax import lax
from jax.sharding import PartitionSpec as P


def with_halo(x, sides, width):
    for axis, dim in sides:
        devices, length = (lax.axis_size(axis), x.shape[dim])
        up = [(i, (i + 1) % devices) for i in range(devices - 1)]
        down = [(j, i) for i, j in up]
        last = lax.slice_in_dim(x, length - width, length, axis=dim)
        first = lax.slice_in_dim(x, 0, width, axis=dim)
        before = lax.ppermute(last, axis, up)
        after = lax.ppermute(first, axis, down)
        x = jnp.concatenate([before, x, after], axis=dim)
    return x


def on_device(cotangent, layer_input, filter_values, weights, row_offset, reach):
    feature_channels, rows, cols = cotangent.shape
    kernels, nlat, span, taps = filter_values.shape
    reach_q = (taps - 1) // 2
    rim = span - 1
    tall = rows + 2 * rim
    first_row = lax.axis_index("lat") * rows
    padded = with_halo(cotangent, (("lat", 1),), rim)
    source = first_row - rim + jnp.arange(tall, dtype=jnp.int32)
    inside = (source >= 0) & (source < nlat)
    safe = jnp.clip(source, 0, nlat - 1)
    offsets = jnp.take(row_offset, safe)
    tap_reach_list = jnp.where(inside, jnp.take(reach, safe), 0)
    psi_rows = jnp.take(filter_values, safe, axis=1).astype(jnp.float32)
    tap_ids = jnp.arange(taps, dtype=jnp.int32) - reach_q
    live = (jnp.abs(tap_ids)[None, :] < tap_reach_list[:, None]).astype(jnp.float32)
    level = (
        jnp.arange(rows, dtype=jnp.int32)[:, None]
        - jnp.arange(tall, dtype=jnp.int32)[None, :]
        + rim
        - offsets[None, :]
    )
    pick = (level[:, :, None] == jnp.arange(span, dtype=jnp.int32)[None, None, :]).astype(
        jnp.float32
    )
    mixing = jnp.einsum("ios,kost->ktio", pick, psi_rows * live[None, :, None, :]).astype(
        jnp.bfloat16
    )
    widest = jnp.max(tap_reach_list)
    lower = reach_q - widest + 1
    upper = reach_q + widest
    moved = lax.all_to_all(padded, "lon", split_axis=0, concat_axis=2, tiled=True)
    wide = jnp.concatenate([moved[:, :, -reach_q:], moved, moved[:, :, :reach_q]], axis=2)
    out_cols = wide.shape[2] - 2 * reach_q
    local_channels = wide.shape[0]

    def add_tap(tap, total):
        shifted = lax.dynamic_slice_in_dim(wide, 2 * reach_q - tap, out_cols, 2)
        mix_tap = lax.dynamic_index_in_dim(mixing, tap, 1, keepdims=False)
        return total + jnp.einsum(
            "kio,col->kcil", mix_tap, shifted, preferred_element_type=jnp.float32
        )

    start = jnp.zeros((kernels, local_channels, rows, out_cols), jnp.float32)
    tap_spread_width = lax.fori_loop(lower, upper, add_tap, start).astype(jnp.bfloat16)
    tap_spread_width = lax.all_to_all(
        tap_spread_width, "lon", split_axis=3, concat_axis=1, tiled=True
    )
    input_grad = lax.dot_general(
        weights, tap_spread_width, (((0, 1), (0, 1)), ((), ())), preferred_element_type=jnp.float32
    )
    partial_grad = lax.dot_general(
        tap_spread_width,
        layer_input,
        (((2, 3), (1, 2)), ((), ())),
        preferred_element_type=jnp.float32,
    )
    total_grad = lax.psum(partial_grad, ("lat", "lon"))
    longitude_count_full = cols * lax.axis_size("lon")
    weight_grad = total_grad / jnp.sqrt(jnp.float32(nlat * longitude_count_full))
    return (input_grad.astype(jnp.bfloat16), weight_grad)


def solution(mesh):
    return jax.shard_map(
        on_device,
        mesh=mesh,
        in_specs=(P(None, "lat", "lon"), P(None, "lat", "lon"), P(), P(), P(), P()),
        out_specs=(P(None, "lat", "lon"), P()),
        check_vma=False,
    )
```

profile of v0, /device:TPU:2, one launch (start us, length us, event | category | flops | bytes accessed | tf_op | source)
XLA Modules:
  0.0 651.0 jit_solution(12407384555351623323)
XLA Ops:
  19.3 7.6 %all-to-all-start = ((bf16[384,18,128]{2,1,0:T(8,128)(2,1)}), bf16[384,18,128]{2,1,0:T(8,128)(2,1)S(1)}, u32[]{:S(2)}, u32[]{:S(2)}) async-start(bf16[384,18,128]{2,1,0:T(8,128)(2,1)} %pad_maximum_fusion), calls=%async_computation | async-start | bytes 4718592 | tf_op jit(solution)/shard_map/all_to_all | solution.py:51
  31.4 2.9 copy.50
  40.9 13.7 %all-to-all-done = bf16[384,18,128]{2,1,0:T(8,128)(2,1)S(1)} async-done(((bf16[384,18,128]{2,1,0:T(8,128)(2,1)}), bf16[384,18,128]{2,1,0:T(8,128)(2,1)S(1)}, u32[]{:S(2)}, u32[]{:S(2)}) %all-to-all-start) | async-done | bytes 1769504 | tf_op jit(solution)/shard_map/all_to_all | solution.py:51
  61.0 4.4 concatenate.7
  65.4 4.8 broadcast_in_dim.17
  70.2 183.5 %while.12 = (s32[]{:T(128)}, f32[3,48,12,1024]{3,2,0,1:T(8,128)}, s32[]{:T(128)}, bf16[48,18,1040]{2,0,1:T(8,128)(2,1)S(1)}, bf16[3,17,12,18]{3,2,0,1:T(8,128)(2...) while((s32[]{:T(128)}, f32[3,48,12,1024]{3,2,0,1:T(8,128)}, s32[]{:T(128)}, ...), condition=%wide.region_2.4_spmd, body=%wide.region_1.3_spmd.sunk | while | flops 65470472 | bytes 21835972 | solution.py:64
  71.0 10.0 %bitcast_add_fusion.2 = f32[3,48,12,1024]{3,2,0,1:T(8,128)} fusion(f32[3,48,12,1024]{3,2,0,1:T(8,128)} %get-tuple-element.167, bf16[48,18,1024]{2,0,1:T(8,128)(2,1)S(1)} %constant_dynamic-slice_fusion.2, bf16[3,17,12,18]{3,2,0,1:T(8,128)(2,1)} %get-tuple-element.180, s32[]{:T(128)S(6)} %select_n.77), kind=kOutput, calls=%fused_computation.3.clone.1 | convolution fusion | flops 65470464 | bytes 18296836 | tf_op jit(solution)/shard_map/while/body/kio,col->kcil/dot_general | solution.py:59
  81.8 10.0 %bitcast_add_fusion.2 = f32[3,48,12,1024]{3,2,0,1:T(8,128)} fusion(f32[3,48,12,1024]{3,2,0,1:T(8,128)} %get-tuple-element.167, bf16[48,18,1024]{2,0,1:T(8,128)(2,1)S(1)} %constant_dynamic-slice_fusion.2, bf16[3,17,12,18]{3,2,0,1:T(8,128)(2,1)} %get-tuple-element.180, s32[]{:T(128)S(6)} %select_n.77), kind=kOutput, calls=%fused_computation.3.clone.1 | convolution fusion | flops 65470464 | bytes 18296836 | tf_op jit(solution)/shard_map/while/body/kio,col->kcil/dot_general | solution.py:59
  92.6 10.0 %bitcast_add_fusion.2 = f32[3,48,12,1024]{3,2,0,1:T(8,128)} fusion(f32[3,48,12,1024]{3,2,0,1:T(8,128)} %get-tuple-element.167, bf16[48,18,1024]{2,0,1:T(8,128)(2,1)S(1)} %constant_dynamic-slice_fusion.2, bf16[3,17,12,18]{3,2,0,1:T(8,128)(2,1)} %get-tuple-element.180, s32[]{:T(128)S(6)} %select_n.77), kind=kOutput, calls=%fused_computation.3.clone.1 | convolution fusion | flops 65470464 | bytes 18296836 | tf_op jit(solution)/shard_map/while/body/kio,col->kcil/dot_general | solution.py:59
  103.4 10.0 %bitcast_add_fusion.2 = f32[3,48,12,1024]{3,2,0,1:T(8,128)} fusion(f32[3,48,12,1024]{3,2,0,1:T(8,128)} %get-tuple-element.167, bf16[48,18,1024]{2,0,1:T(8,128)(2,1)S(1)} %constant_dynamic-slice_fusion.2, bf16[3,17,12,18]{3,2,0,1:T(8,128)(2,1)} %get-tuple-element.180, s32[]{:T(128)S(6)} %select_n.77), kind=kOutput, calls=%fused_computation.3.clone.1 | convolution fusion | flops 65470464 | bytes 18296836 | tf_op jit(solution)/shard_map/while/body/kio,col->kcil/dot_general | solution.py:59
  114.2 10.0 %bitcast_add_fusion.2 = f32[3,48,12,1024]{3,2,0,1:T(8,128)} fusion(f32[3,48,12,1024]{3,2,0,1:T(8,128)} %get-tuple-element.167, bf16[48,18,1024]{2,0,1:T(8,128)(2,1)S(1)} %constant_dynamic-slice_fusion.2, bf16[3,17,12,18]{3,2,0,1:T(8,128)(2,1)} %get-tuple-element.180, s32[]{:T(128)S(6)} %select_n.77), kind=kOutput, calls=%fused_computation.3.clone.1 | convolution fusion | flops 65470464 | bytes 18296836 | tf_op jit(solution)/shard_map/while/body/kio,col->kcil/dot_general | solution.py:59
  125.0 10.0 %bitcast_add_fusion.2 = f32[3,48,12,1024]{3,2,0,1:T(8,128)} fusion(f32[3,48,12,1024]{3,2,0,1:T(8,128)} %get-tuple-element.167, bf16[48,18,1024]{2,0,1:T(8,128)(2,1)S(1)} %constant_dynamic-slice_fusion.2, bf16[3,17,12,18]{3,2,0,1:T(8,128)(2,1)} %get-tuple-element.180, s32[]{:T(128)S(6)} %select_n.77), kind=kOutput, calls=%fused_computation.3.clone.1 | convolution fusion | flops 65470464 | bytes 18296836 | tf_op jit(solution)/shard_map/while/body/kio,col->kcil/dot_general | solution.py:59
  135.8 10.0 %bitcast_add_fusion.2 = f32[3,48,12,1024]{3,2,0,1:T(8,128)} fusion(f32[3,48,12,1024]{3,2,0,1:T(8,128)} %get-tuple-element.167, bf16[48,18,1024]{2,0,1:T(8,128)(2,1)S(1)} %constant_dynamic-slice_fusion.2, bf16[3,17,12,18]{3,2,0,1:T(8,128)(2,1)} %get-tuple-element.180, s32[]{:T(128)S(6)} %select_n.77), kind=kOutput, calls=%fused_computation.3.clone.1 | convolution fusion | flops 65470464 | bytes 18296836 | tf_op jit(solution)/shard_map/while/body/kio,col->kcil/dot_general | solution.py:59
  146.6 10.0 %bitcast_add_fusion.2 = f32[3,48,12,1024]{3,2,0,1:T(8,128)} fusion(f32[3,48,12,1024]{3,2,0,1:T(8,128)} %get-tuple-element.167, bf16[48,18,1024]{2,0,1:T(8,128)(2,1)S(1)} %constant_dynamic-slice_fusion.2, bf16[3,17,12,18]{3,2,0,1:T(8,128)(2,1)} %get-tuple-element.180, s32[]{:T(128)S(6)} %select_n.77), kind=kOutput, calls=%fused_computation.3.clone.1 | convolution fusion | flops 65470464 | bytes 18296836 | tf_op jit(solution)/shard_map/while/body/kio,col->kcil/dot_general | solution.py:59
  157.4 10.0 %bitcast_add_fusion.2 = f32[3,48,12,1024]{3,2,0,1:T(8,128)} fusion(f32[3,48,12,1024]{3,2,0,1:T(8,128)} %get-tuple-element.167, bf16[48,18,1024]{2,0,1:T(8,128)(2,1)S(1)} %constant_dynamic-slice_fusion.2, bf16[3,17,12,18]{3,2,0,1:T(8,128)(2,1)} %get-tuple-element.180, s32[]{:T(128)S(6)} %select_n.77), kind=kOutput, calls=%fused_computation.3.clone.1 | convolution fusion | flops 65470464 | bytes 18296836 | tf_op jit(solution)/shard_map/while/body/kio,col->kcil/dot_general | solution.py:59
  168.1 10.0 %bitcast_add_fusion.2 = f32[3,48,12,1024]{3,2,0,1:T(8,128)} fusion(f32[3,48,12,1024]{3,2,0,1:T(8,128)} %get-tuple-element.167, bf16[48,18,1024]{2,0,1:T(8,128)(2,1)S(1)} %constant_dynamic-slice_fusion.2, bf16[3,17,12,18]{3,2,0,1:T(8,128)(2,1)} %get-tuple-element.180, s32[]{:T(128)S(6)} %select_n.77), kind=kOutput, calls=%fused_computation.3.clone.1 | convolution fusion | flops 65470464 | bytes 18296836 | tf_op jit(solution)/shard_map/while/body/kio,col->kcil/dot_general | solution.py:59
  178.9 10.0 %bitcast_add_fusion.2 = f32[3,48,12,1024]{3,2,0,1:T(8,128)} fusion(f32[3,48,12,1024]{3,2,0,1:T(8,128)} %get-tuple-element.167, bf16[48,18,1024]{2,0,1:T(8,128)(2,1)S(1)} %constant_dynamic-slice_fusion.2, bf16[3,17,12,18]{3,2,0,1:T(8,128)(2,1)} %get-tuple-element.180, s32[]{:T(128)S(6)} %select_n.77), kind=kOutput, calls=%fused_computation.3.clone.1 | convolution fusion | flops 65470464 | bytes 18296836 | tf_op jit(solution)/shard_map/while/body/kio,col->kcil/dot_general | solution.py:59
  189.7 10.0 %bitcast_add_fusion.2 = f32[3,48,12,1024]{3,2,0,1:T(8,128)} fusion(f32[3,48,12,1024]{3,2,0,1:T(8,128)} %get-tuple-element.167, bf16[48,18,1024]{2,0,1:T(8,128)(2,1)S(1)} %constant_dynamic-slice_fusion.2, bf16[3,17,12,18]{3,2,0,1:T(8,128)(2,1)} %get-tuple-element.180, s32[]{:T(128)S(6)} %select_n.77), kind=kOutput, calls=%fused_computation.3.clone.1 | convolution fusion | flops 65470464 | bytes 18296836 | tf_op jit(solution)/shard_map/while/body/kio,col->kcil/dot_general | solution.py:59
  200.5 10.0 %bitcast_add_fusion.2 = f32[3,48,12,1024]{3,2,0,1:T(8,128)} fusion(f32[3,48,12,1024]{3,2,0,1:T(8,128)} %get-tuple-element.167, bf16[48,18,1024]{2,0,1:T(8,128)(2,1)S(1)} %constant_dynamic-slice_fusion.2, bf16[3,17,12,18]{3,2,0,1:T(8,128)(2,1)} %get-tuple-element.180, s32[]{:T(128)S(6)} %select_n.77), kind=kOutput, calls=%fused_computation.3.clone.1 | convolution fusion | flops 65470464 | bytes 18296836 | tf_op jit(solution)/shard_map/while/body/kio,col->kcil/dot_general | solution.py:59
  211.3 10.0 %bitcast_add_fusion.2 = f32[3,48,12,1024]{3,2,0,1:T(8,128)} fusion(f32[3,48,12,1024]{3,2,0,1:T(8,128)} %get-tuple-element.167, bf16[48,18,1024]{2,0,1:T(8,128)(2,1)S(1)} %constant_dynamic-slice_fusion.2, bf16[3,17,12,18]{3,2,0,1:T(8,128)(2,1)} %get-tuple-element.180, s32[]{:T(128)S(6)} %select_n.77), kind=kOutput, calls=%fused_computation.3.clone.1 | convolution fusion | flops 65470464 | bytes 18296836 | tf_op jit(solution)/shard_map/while/body/kio,col->kcil/dot_general | solution.py:59
  222.1 10.0 %bitcast_add_fusion.2 = f32[3,48,12,1024]{3,2,0,1:T(8,128)} fusion(f32[3,48,12,1024]{3,2,0,1:T(8,128)} %get-tuple-element.167, bf16[48,18,1024]{2,0,1:T(8,128)(2,1)S(1)} %constant_dynamic-slice_fusion.2, bf16[3,17,12,18]{3,2,0,1:T(8,128)(2,1)} %get-tuple-element.180, s32[]{:T(128)S(6)} %select_n.77), kind=kOutput, calls=%fused_computation.3.clone.1 | convolution fusion | flops 65470464 | bytes 18296836 | tf_op jit(solution)/shard_map/while/body/kio,col->kcil/dot_general | solution.py:59
  232.9 10.0 %bitcast_add_fusion.2 = f32[3,48,12,1024]{3,2,0,1:T(8,128)} fusion(f32[3,48,12,1024]{3,2,0,1:T(8,128)} %get-tuple-element.167, bf16[48,18,1024]{2,0,1:T(8,128)(2,1)S(1)} %constant_dynamic-slice_fusion.2, bf16[3,17,12,18]{3,2,0,1:T(8,128)(2,1)} %get-tuple-element.180, s32[]{:T(128)S(6)} %select_n.77), kind=kOutput, calls=%fused_computation.3.clone.1 | convolution fusion | flops 65470464 | bytes 18296836 | tf_op jit(solution)/shard_map/while/body/kio,col->kcil/dot_general | solution.py:59
  243.7 10.0 %bitcast_add_fusion.2 = f32[3,48,12,1024]{3,2,0,1:T(8,128)} fusion(f32[3,48,12,1024]{3,2,0,1:T(8,128)} %get-tuple-element.167, bf16[48,18,1024]{2,0,1:T(8,128)(2,1)S(1)} %constant_dynamic-slice_fusion.2, bf16[3,17,12,18]{3,2,0,1:T(8,128)(2,1)} %get-tuple-element.180, s32[]{:T(128)S(6)} %select_n.77), kind=kOutput, calls=%fused_computation.3.clone.1 | convolution fusion | flops 65470464 | bytes 18296836 | tf_op jit(solution)/shard_map/while/body/kio,col->kcil/dot_general | solution.py:59
  253.7 9.2 %copy.71 = bf16[3,48,12,1024]{3,1,2,0:T(8,128)(2,1)} copy(f32[3,48,12,1024]{3,2,0,1:T(8,128)} %get-tuple-element.71) | data formatting | bytes 10616832 | tf_op jit(solution)/shard_map/while | solution.py:64
  262.9 14.4 %copy.54 = bf16[3,48,12,1024]{1,2,0,3:T(8,128)(2,1)} copy(bf16[3,48,12,1024]{3,1,2,0:T(8,128)(2,1)} %copy.71) | data formatting | bytes 7077888 | tf_op jit(solution)/shard_map/convert_element_type | solution.py:64
  277.3 16.4 %reshape.127 = bf16[8,2,110592]{2,1,0:T(2,128)(2,1)} reshape(bf16[1024,3,12,48]{3,2,1,0:T(8,128)(2,1)} %bitcast.63) | data formatting | bytes 7077888
  293.8 52.3 %all_to_all.36 = bf16[8,2,110592]{2,1,0:T(2,128)(2,1)} all-to-all(bf16[8,2,110592]{2,1,0:T(2,128)(2,1)} %reshape.127), channel_id=1, replica_groups=mesh['lat'=32,'lon'=8] {'lon'}, dimensions={0} | all-to-all | bytes 7077888 | tf_op jit(solution)/shard_map/all_to_all | solution.py:65
  346.1 17.7 %reshape.128 = bf16[1024,3,12,48]{3,2,1,0:T(8,128)(2,1)} reshape(bf16[8,2,110592]{2,1,0:T(2,128)(2,1)} %all_to_all.36) | data formatting | bytes 7077888
  363.8 13.7 %copy.56 = bf16[3,8,48,12,128]{4,2,1,3,0:T(8,128)(2,1)} copy(bf16[3,8,48,12,128]{2,3,0,4,1:T(8,128)(2,1)} %bitcast.64) | data formatting | bytes 7077888 | tf_op jit(solution)/shard_map/all_to_all | solution.py:65
  377.5 5.3 convolution_bitcast_fusion
  382.9 4.2 fusion.3
  388.5 252.8 %all-reduce.2.cloned.1.call-done = f32[3,384,384]{2,1,0:T(8,128)} async-done(((f32[3,384,384]{2,1,0:T(8,128)}), f32[3,384,384]{2,1,0:T(8,128)}) %all-reduce.2.cloned.1.call-update) | async-done | bytes 1769488 | tf_op jit(solution)/shard_map/psum | solution.py:77
  (57 shorter events, 46.1 us)
Async XLA Ops:
  7.2 370.4 %copy-start = (bf16[384,12,128]{2,0,1:T(8,128)(2,1)S(1)}, bf16[384,12,128]{2,0,1:T(8,128)(2,1)}, u32[]{:S(2)}) copy-start(bf16[384,12,128]{2,0,1:T(8,128)(2,1)} %param.11) | copy-start | bytes 3538948
  9.1 5.8 collective-permute-start
  11.5 4.6 collective-permute-start.1
  19.3 7.6 %copy-start.1 = (s32[384]{0:T(512)S(1)}, s32[384]{0:T(512)}, u32[]{:S(2)}) copy-start(s32[384]{0:T(512)} %param.14) | copy-start | bytes 4612
  19.3 8.3 %copy-start.2 = (s32[384]{0:T(512)S(1)}, s32[384]{0:T(512)}, u32[]{:S(2)}) copy-start(s32[384]{0:T(512)} %param.15) | copy-start | bytes 4612
  19.3 35.4 %all-to-all-start = ((bf16[384,18,128]{2,1,0:T(8,128)(2,1)}), bf16[384,18,128]{2,1,0:T(8,128)(2,1)S(1)}, u32[]{:S(2)}, u32[]{:S(2)}) async-start(bf16[384,18,128]{2,1,0:T(8,128)(2,1)} %pad_maximum_fusion), calls=%async_computation | async-start | bytes 4718592 | tf_op jit(solution)/shard_map/all_to_all | solution.py:51
  26.9 614.5 %all-reduce.2.cloned.1.call-start = ((), (), s32[]{:S(2)}) async-start(), calls=%async_computation.2 | async-start | bytes 3538944 | tf_op jit(solution)/shard_map/psum | solution.py:77
  59.7 1.3 copy-start.3
  377.5 5.3 copy-start.4
Sparse Core Ops, SparseCore 0:
  383.0 258.2 all-reduce.1
where the time goes:
time: 653 us; the launch traced here: 651 us
  waiting for transfers between devices  267 us (41%)
  matrix products  181 us (28%)
  local copies, waits for them, and re-layouts  117 us (18%)
  blocking collectives  52.3 us (8%)
  between operations  15.5 us (2%)
  starting transfers between devices  11.3 us (2%)
  other arithmetic  7.17 us (1%)
    psum x1, waiting for transfers between devices, on_device(): total_grad = lax.psum(partial_grad, ('lat', 'lon'))  253 us
    dot_general x17, matrix products, add_tap(): jnp.einsum('kio,col->kcil', mix_tap, shifted, preferred_element_type=jnp....  170 us
    all_to_all x1, blocking collectives, on_device(): lax.all_to_all(tap_spread_width, 'lon', split_axis=3, concat_axis=1, tile...  52.3 us
    unnamed x15, local copies, waits for them, and re-layouts  41 us
    convert_element_type x1, local copies, waits for them, and re-layouts, on_device(): lax.fori_loop(lower, upper, add_tap, start).astype(jnp.bfloat16)  14.4 us
    all_to_all x1, waiting for transfers between devices, on_device(): lax.all_to_all(padded, 'lon', split_axis=0, concat_axis=2, tiled=True)  13.7 us
    all_to_all x1, local copies, waits for them, and re-layouts, on_device(): lax.all_to_all(tap_spread_width, 'lon', split_axis=3, concat_axis=1, tile...  13.7 us
    dynamic_slice x17, local copies, waits for them, and re-layouts, add_tap(): shifted = lax.dynamic_slice_in_dim(wide, 2 * reach_q - tap, out_cols, 2)  13.6 us
  transfers between devices with their start and end apart: 4, of which 2 were waited for; matrix products, arithmetic and copies ran while one was open for 3% of the time, Pallas kernels for 0%

commit v1 on v0

--- a/solution.py
+++ b/solution.py
@@ -74,7 +74,7 @@
         (((2, 3), (1, 2)), ((), ())),
         preferred_element_type=jnp.float32,
     )
-    total_grad = lax.psum(partial_grad, ("lat", "lon"))
+    total_grad = lax.psum(lax.psum(partial_grad, "lon"), "lat")
     longitude_count_full = cols * lax.axis_size("lon")
     weight_grad = total_grad / jnp.sqrt(jnp.float32(nlat * longitude_count_full))
     return (input_grad.astype(jnp.bfloat16), weight_grad)

time: 653 us -> 716 us (1.096)
  waiting for transfers between devices: 267 us -> 330 us
    psum x1 -> x2, waiting for transfers between devices: 253 us -> 316 us  [on_device(): total_grad = lax.psum(lax.psum(partial_grad, 'lon'), 'lat')]
  transfers between devices with their start and end apart: 4 -> 5, of which waited for: 2 -> 3; matrix products, arithmetic and copies ran while one was open for 3% -> 3% of each run, Pallas kernels for 0% -> 0%
where the time goes in v1:
time: 716 us; the launch traced here: 714 us
  waiting for transfers between devices  330 us (46%)
  matrix products  181 us (25%)
  local copies, waits for them, and re-layouts  117 us (16%)
  blocking collectives  52.3 us (7%)
  between operations  15.5 us (2%)
  starting transfers between devices  11.6 us (2%)
  other arithmetic  7.17 us (1%)
    psum x2, waiting for transfers between devices, on_device(): total_grad = lax.psum(lax.psum(partial_grad, 'lon'), 'lat')  316 us
    dot_general x17, matrix products, add_tap(): jnp.einsum('kio,col->kcil', mix_tap, shifted, preferred_element_type=jnp....  170 us
    all_to_all x1, blocking collectives, on_device(): lax.all_to_all(tap_spread_width, 'lon', split_axis=3, concat_axis=1, tile...  52.3 us
    unnamed x15, local copies, waits for them, and re-layouts  41 us
    convert_element_type x1, local copies, waits for them, and re-layouts, on_device(): lax.fori_loop(lower, upper, add_tap, start).astype(jnp.bfloat16)  14.4 us
  transfers between devices with their start and end apart: 5, of which 3 were waited for; matrix products, arithmetic and copies ran while one was open for 3% of the time, Pallas kernels for 0%

profile of v1, /device:TPU:2, one launch (start us, length us, event | category | flops | bytes accessed | tf_op | source)
XLA Modules:
  0.0 714.2 jit_solution(11441902894461088198)
XLA Ops:
  19.3 7.6 %all-to-all-start = ((bf16[384,18,128]{2,1,0:T(8,128)(2,1)}), bf16[384,18,128]{2,1,0:T(8,128)(2,1)S(1)}, u32[]{:S(2)}, u32[]{:S(2)}) async-start(bf16[384,18,128]{2,1,0:T(8,128)(2,1)} %pad_maximum_fusion), calls=%async_computation | async-start | bytes 4718592 | tf_op jit(solution)/shard_map/all_to_all | solution.py:51
  40.9 13.7 %all-to-all-done = bf16[384,18,128]{2,1,0:T(8,128)(2,1)S(1)} async-done(((bf16[384,18,128]{2,1,0:T(8,128)(2,1)}), bf16[384,18,128]{2,1,0:T(8,128)(2,1)S(1)}, u32[]{:S(2)}, u32[]{:S(2)}) %all-to-all-start) | async-done | bytes 1769504 | tf_op jit(solution)/shard_map/all_to_all | solution.py:51
  61.0 4.4 concatenate.7
  65.4 4.8 broadcast_in_dim.17
  70.2 183.4 %while.12 = (s32[]{:T(128)}, f32[3,48,12,1024]{3,2,0,1:T(8,128)}, s32[]{:T(128)}, bf16[48,18,1040]{2,0,1:T(8,128)(2,1)S(1)}, bf16[3,17,12,18]{3,2,0,1:T(8,128)(2...) while((s32[]{:T(128)}, f32[3,48,12,1024]{3,2,0,1:T(8,128)}, s32[]{:T(128)}, ...), condition=%wide.region_2.4_spmd, body=%wide.region_1.3_spmd.sunk | while | flops 65470472 | bytes 21835972 | solution.py:64
  71.0 10.0 %bitcast_add_fusion.2 = f32[3,48,12,1024]{3,2,0,1:T(8,128)} fusion(f32[3,48,12,1024]{3,2,0,1:T(8,128)} %get-tuple-element.167, bf16[48,18,1024]{2,0,1:T(8,128)(2,1)S(1)} %constant_dynamic-slice_fusion.2, bf16[3,17,12,18]{3,2,0,1:T(8,128)(2,1)} %get-tuple-element.180, s32[]{:T(128)S(6)} %select_n.77), kind=kOutput, calls=%fused_computation.3.clone.1 | convolution fusion | flops 65470464 | bytes 18296836 | tf_op jit(solution)/shard_map/while/body/kio,col->kcil/dot_general | solution.py:59
  81.8 10.0 %bitcast_add_fusion.2 = f32[3,48,12,1024]{3,2,0,1:T(8,128)} fusion(f32[3,48,12,1024]{3,2,0,1:T(8,128)} %get-tuple-element.167, bf16[48,18,1024]{2,0,1:T(8,128)(2,1)S(1)} %constant_dynamic-slice_fusion.2, bf16[3,17,12,18]{3,2,0,1:T(8,128)(2,1)} %get-tuple-element.180, s32[]{:T(128)S(6)} %select_n.77), kind=kOutput, calls=%fused_computation.3.clone.1 | convolution fusion | flops 65470464 | bytes 18296836 | tf_op jit(solution)/shard_map/while/body/kio,col->kcil/dot_general | solution.py:59
  92.6 10.0 %bitcast_add_fusion.2 = f32[3,48,12,1024]{3,2,0,1:T(8,128)} fusion(f32[3,48,12,1024]{3,2,0,1:T(8,128)} %get-tuple-element.167, bf16[48,18,1024]{2,0,1:T(8,128)(2,1)S(1)} %constant_dynamic-slice_fusion.2, bf16[3,17,12,18]{3,2,0,1:T(8,128)(2,1)} %get-tuple-element.180, s32[]{:T(128)S(6)} %select_n.77), kind=kOutput, calls=%fused_computation.3.clone.1 | convolution fusion | flops 65470464 | bytes 18296836 | tf_op jit(solution)/shard_map/while/body/kio,col->kcil/dot_general | solution.py:59
  103.4 10.0 %bitcast_add_fusion.2 = f32[3,48,12,1024]{3,2,0,1:T(8,128)} fusion(f32[3,48,12,1024]{3,2,0,1:T(8,128)} %get-tuple-element.167, bf16[48,18,1024]{2,0,1:T(8,128)(2,1)S(1)} %constant_dynamic-slice_fusion.2, bf16[3,17,12,18]{3,2,0,1:T(8,128)(2,1)} %get-tuple-element.180, s32[]{:T(128)S(6)} %select_n.77), kind=kOutput, calls=%fused_computation.3.clone.1 | convolution fusion | flops 65470464 | bytes 18296836 | tf_op jit(solution)/shard_map/while/body/kio,col->kcil/dot_general | solution.py:59
  114.2 10.0 %bitcast_add_fusion.2 = f32[3,48,12,1024]{3,2,0,1:T(8,128)} fusion(f32[3,48,12,1024]{3,2,0,1:T(8,128)} %get-tuple-element.167, bf16[48,18,1024]{2,0,1:T(8,128)(2,1)S(1)} %constant_dynamic-slice_fusion.2, bf16[3,17,12,18]{3,2,0,1:T(8,128)(2,1)} %get-tuple-element.180, s32[]{:T(128)S(6)} %select_n.77), kind=kOutput, calls=%fused_computation.3.clone.1 | convolution fusion | flops 65470464 | bytes 18296836 | tf_op jit(solution)/shard_map/while/body/kio,col->kcil/dot_general | solution.py:59
  125.0 10.0 %bitcast_add_fusion.2 = f32[3,48,12,1024]{3,2,0,1:T(8,128)} fusion(f32[3,48,12,1024]{3,2,0,1:T(8,128)} %get-tuple-element.167, bf16[48,18,1024]{2,0,1:T(8,128)(2,1)S(1)} %constant_dynamic-slice_fusion.2, bf16[3,17,12,18]{3,2,0,1:T(8,128)(2,1)} %get-tuple-element.180, s32[]{:T(128)S(6)} %select_n.77), kind=kOutput, calls=%fused_computation.3.clone.1 | convolution fusion | flops 65470464 | bytes 18296836 | tf_op jit(solution)/shard_map/while/body/kio,col->kcil/dot_general | solution.py:59
  135.8 10.0 %bitcast_add_fusion.2 = f32[3,48,12,1024]{3,2,0,1:T(8,128)} fusion(f32[3,48,12,1024]{3,2,0,1:T(8,128)} %get-tuple-element.167, bf16[48,18,1024]{2,0,1:T(8,128)(2,1)S(1)} %constant_dynamic-slice_fusion.2, bf16[3,17,12,18]{3,2,0,1:T(8,128)(2,1)} %get-tuple-element.180, s32[]{:T(128)S(6)} %select_n.77), kind=kOutput, calls=%fused_computation.3.clone.1 | convolution fusion | flops 65470464 | bytes 18296836 | tf_op jit(solution)/shard_map/while/body/kio,col->kcil/dot_general | solution.py:59
  146.6 10.0 %bitcast_add_fusion.2 = f32[3,48,12,1024]{3,2,0,1:T(8,128)} fusion(f32[3,48,12,1024]{3,2,0,1:T(8,128)} %get-tuple-element.167, bf16[48,18,1024]{2,0,1:T(8,128)(2,1)S(1)} %constant_dynamic-slice_fusion.2, bf16[3,17,12,18]{3,2,0,1:T(8,128)(2,1)} %get-tuple-element.180, s32[]{:T(128)S(6)} %select_n.77), kind=kOutput, calls=%fused_computation.3.clone.1 | convolution fusion | flops 65470464 | bytes 18296836 | tf_op jit(solution)/shard_map/while/body/kio,col->kcil/dot_general | solution.py:59
  157.3 10.0 %bitcast_add_fusion.2 = f32[3,48,12,1024]{3,2,0,1:T(8,128)} fusion(f32[3,48,12,1024]{3,2,0,1:T(8,128)} %get-tuple-element.167, bf16[48,18,1024]{2,0,1:T(8,128)(2,1)S(1)} %constant_dynamic-slice_fusion.2, bf16[3,17,12,18]{3,2,0,1:T(8,128)(2,1)} %get-tuple-element.180, s32[]{:T(128)S(6)} %select_n.77), kind=kOutput, calls=%fused_computation.3.clone.1 | convolution fusion | flops 65470464 | bytes 18296836 | tf_op jit(solution)/shard_map/while/body/kio,col->kcil/dot_general | solution.py:59
  168.1 10.0 %bitcast_add_fusion.2 = f32[3,48,12,1024]{3,2,0,1:T(8,128)} fusion(f32[3,48,12,1024]{3,2,0,1:T(8,128)} %get-tuple-element.167, bf16[48,18,1024]{2,0,1:T(8,128)(2,1)S(1)} %constant_dynamic-slice_fusion.2, bf16[3,17,12,18]{3,2,0,1:T(8,128)(2,1)} %get-tuple-element.180, s32[]{:T(128)S(6)} %select_n.77), kind=kOutput, calls=%fused_computation.3.clone.1 | convolution fusion | flops 65470464 | bytes 18296836 | tf_op jit(solution)/shard_map/while/body/kio,col->kcil/dot_general | solution.py:59
  178.9 10.0 %bitcast_add_fusion.2 = f32[3,48,12,1024]{3,2,0,1:T(8,128)} fusion(f32[3,48,12,1024]{3,2,0,1:T(8,128)} %get-tuple-element.167, bf16[48,18,1024]{2,0,1:T(8,128)(2,1)S(1)} %constant_dynamic-slice_fusion.2, bf16[3,17,12,18]{3,2,0,1:T(8,128)(2,1)} %get-tuple-element.180, s32[]{:T(128)S(6)} %select_n.77), kind=kOutput, calls=%fused_computation.3.clone.1 | convolution fusion | flops 65470464 | bytes 18296836 | tf_op jit(solution)/shard_map/while/body/kio,col->kcil/dot_general | solution.py:59
  189.7 10.0 %bitcast_add_fusion.2 = f32[3,48,12,1024]{3,2,0,1:T(8,128)} fusion(f32[3,48,12,1024]{3,2,0,1:T(8,128)} %get-tuple-element.167, bf16[48,18,1024]{2,0,1:T(8,128)(2,1)S(1)} %constant_dynamic-slice_fusion.2, bf16[3,17,12,18]{3,2,0,1:T(8,128)(2,1)} %get-tuple-element.180, s32[]{:T(128)S(6)} %select_n.77), kind=kOutput, calls=%fused_computation.3.clone.1 | convolution fusion | flops 65470464 | bytes 18296836 | tf_op jit(solution)/shard_map/while/body/kio,col->kcil/dot_general | solution.py:59
  200.5 10.0 %bitcast_add_fusion.2 = f32[3,48,12,1024]{3,2,0,1:T(8,128)} fusion(f32[3,48,12,1024]{3,2,0,1:T(8,128)} %get-tuple-element.167, bf16[48,18,1024]{2,0,1:T(8,128)(2,1)S(1)} %constant_dynamic-slice_fusion.2, bf16[3,17,12,18]{3,2,0,1:T(8,128)(2,1)} %get-tuple-element.180, s32[]{:T(128)S(6)} %select_n.77), kind=kOutput, calls=%fused_computation.3.clone.1 | convolution fusion | flops 65470464 | bytes 18296836 | tf_op jit(solution)/shard_map/while/body/kio,col->kcil/dot_general | solution.py:59
  211.3 10.0 %bitcast_add_fusion.2 = f32[3,48,12,1024]{3,2,0,1:T(8,128)} fusion(f32[3,48,12,1024]{3,2,0,1:T(8,128)} %get-tuple-element.167, bf16[48,18,1024]{2,0,1:T(8,128)(2,1)S(1)} %constant_dynamic-slice_fusion.2, bf16[3,17,12,18]{3,2,0,1:T(8,128)(2,1)} %get-tuple-element.180, s32[]{:T(128)S(6)} %select_n.77), kind=kOutput, calls=%fused_computation.3.clone.1 | convolution fusion | flops 65470464 | bytes 18296836 | tf_op jit(solution)/shard_map/while/body/kio,col->kcil/dot_general | solution.py:59
  222.1 10.0 %bitcast_add_fusion.2 = f32[3,48,12,1024]{3,2,0,1:T(8,128)} fusion(f32[3,48,12,1024]{3,2,0,1:T(8,128)} %get-tuple-element.167, bf16[48,18,1024]{2,0,1:T(8,128)(2,1)S(1)} %constant_dynamic-slice_fusion.2, bf16[3,17,12,18]{3,2,0,1:T(8,128)(2,1)} %get-tuple-element.180, s32[]{:T(128)S(6)} %select_n.77), kind=kOutput, calls=%fused_computation.3.clone.1 | convolution fusion | flops 65470464 | bytes 18296836 | tf_op jit(solution)/shard_map/while/body/kio,col->kcil/dot_general | solution.py:59
  232.9 10.0 %bitcast_add_fusion.2 = f32[3,48,12,1024]{3,2,0,1:T(8,128)} fusion(f32[3,48,12,1024]{3,2,0,1:T(8,128)} %get-tuple-element.167, bf16[48,18,1024]{2,0,1:T(8,128)(2,1)S(1)} %constant_dynamic-slice_fusion.2, bf16[3,17,12,18]{3,2,0,1:T(8,128)(2,1)} %get-tuple-element.180, s32[]{:T(128)S(6)} %select_n.77), kind=kOutput, calls=%fused_computation.3.clone.1 | convolution fusion | flops 65470464 | bytes 18296836 | tf_op jit(solution)/shard_map/while/body/kio,col->kcil/dot_general | solution.py:59
  243.7 10.0 %bitcast_add_fusion.2 = f32[3,48,12,1024]{3,2,0,1:T(8,128)} fusion(f32[3,48,12,1024]{3,2,0,1:T(8,128)} %get-tuple-element.167, bf16[48,18,1024]{2,0,1:T(8,128)(2,1)S(1)} %constant_dynamic-slice_fusion.2, bf16[3,17,12,18]{3,2,0,1:T(8,128)(2,1)} %get-tuple-element.180, s32[]{:T(128)S(6)} %select_n.77), kind=kOutput, calls=%fused_computation.3.clone.1 | convolution fusion | flops 65470464 | bytes 18296836 | tf_op jit(solution)/shard_map/while/body/kio,col->kcil/dot_general | solution.py:59
  253.6 9.2 %copy.71 = bf16[3,48,12,1024]{3,1,2,0:T(8,128)(2,1)} copy(f32[3,48,12,1024]{3,2,0,1:T(8,128)} %get-tuple-element.71) | data formatting | bytes 10616832 | tf_op jit(solution)/shard_map/while | solution.py:64
  262.8 14.4 %copy.54 = bf16[3,48,12,1024]{1,2,0,3:T(8,128)(2,1)} copy(bf16[3,48,12,1024]{3,1,2,0:T(8,128)(2,1)} %copy.71) | data formatting | bytes 7077888 | tf_op jit(solution)/shard_map/convert_element_type | solution.py:64
  277.3 16.4 %reshape.127 = bf16[8,2,110592]{2,1,0:T(2,128)(2,1)} reshape(bf16[1024,3,12,48]{3,2,1,0:T(8,128)(2,1)} %bitcast.63) | data formatting | bytes 7077888
  293.7 52.3 %all_to_all.36 = bf16[8,2,110592]{2,1,0:T(2,128)(2,1)} all-to-all(bf16[8,2,110592]{2,1,0:T(2,128)(2,1)} %reshape.127), channel_id=1, replica_groups=mesh['lat'=32,'lon'=8] {'lon'}, dimensions={0} | all-to-all | bytes 7077888 | tf_op jit(solution)/shard_map/all_to_all | solution.py:65
  346.0 17.7 %reshape.128 = bf16[1024,3,12,48]{3,2,1,0:T(8,128)(2,1)} reshape(bf16[8,2,110592]{2,1,0:T(2,128)(2,1)} %all_to_all.36) | data formatting | bytes 7077888
  363.8 13.7 %copy.56 = bf16[3,8,48,12,128]{4,2,1,3,0:T(8,128)(2,1)} copy(bf16[3,8,48,12,128]{2,3,0,4,1:T(8,128)(2,1)} %bitcast.64) | data formatting | bytes 7077888 | tf_op jit(solution)/shard_map/all_to_all | solution.py:65
  377.5 5.2 convolution_bitcast_fusion
  383.0 91.1 %all-reduce.3.cloned.1.call-done = f32[3,384,384]{2,1,0:T(8,128)} async-done(((f32[3,384,384]{2,1,0:T(8,128)}), f32[3,384,384]{2,1,0:T(8,128)}) %all-reduce.3.cloned.1.call-update) | async-done | bytes 1769488 | tf_op jit(solution)/shard_map/psum | solution.py:77
  474.1 4.2 fusion.3
  479.7 224.8 %all-reduce.5.cloned.1.call-done = f32[3,384,384]{2,1,0:T(8,128)} async-done(((f32[3,384,384]{2,1,0:T(8,128)}), f32[3,384,384]{2,1,0:T(8,128)}) %all-reduce.5.cloned.1.call-update) | async-done | bytes 1769488 | tf_op jit(solution)/shard_map/psum | solution.py:77
  (60 shorter events, 49.3 us)
Async XLA Ops:
  7.2 370.3 %copy-start = (bf16[384,12,128]{2,0,1:T(8,128)(2,1)S(1)}, bf16[384,12,128]{2,0,1:T(8,128)(2,1)}, u32[]{:S(2)}) copy-start(bf16[384,12,128]{2,0,1:T(8,128)(2,1)} %param.11) | copy-start | bytes 3538948
  9.1 5.8 collective-permute-start
  11.5 4.6 collective-permute-start.1
  19.3 7.6 %copy-start.1 = (s32[384]{0:T(512)S(1)}, s32[384]{0:T(512)}, u32[]{:S(2)}) copy-start(s32[384]{0:T(512)} %param.14) | copy-start | bytes 4612
  19.3 8.3 %copy-start.2 = (s32[384]{0:T(512)S(1)}, s32[384]{0:T(512)}, u32[]{:S(2)}) copy-start(s32[384]{0:T(512)} %param.15) | copy-start | bytes 4612
  19.3 35.4 %all-to-all-start = ((bf16[384,18,128]{2,1,0:T(8,128)(2,1)}), bf16[384,18,128]{2,1,0:T(8,128)(2,1)S(1)}, u32[]{:S(2)}, u32[]{:S(2)}) async-start(bf16[384,18,128]{2,1,0:T(8,128)(2,1)} %pad_maximum_fusion), calls=%async_computation | async-start | bytes 4718592 | tf_op jit(solution)/shard_map/all_to_all | solution.py:51
  26.9 447.2 %all-reduce.3.cloned.1.call-start = ((), (), s32[]{:S(2)}) async-start(), calls=%async_computation.2 | async-start | bytes 3538944 | tf_op jit(solution)/shard_map/psum | solution.py:77
  59.7 1.3 copy-start.3
  382.7 91.4 %copy-start.4 = (bf16[3,384,384]{2,1,0:T(8,128)(2,1)S(1)}, bf16[3,384,384]{2,1,0:T(8,128)(2,1)}, u32[]{:S(2)}) copy-start(bf16[3,384,384]{2,1,0:T(8,128)(2,1)} %param.13) | copy-start | bytes 2654212
  382.7 321.8 %all-reduce.5.cloned.1.call-start = ((), (), s32[]{:S(2)}) async-start(), calls=%async_computation.3 | async-start | bytes 3538944 | tf_op jit(solution)/shard_map/psum | solution.py:77
Sparse Core Ops, SparseCore 0:
  382.9 91.1 all-reduce.2
  476.7 227.7 all-reduce.4
